TPU v7x, 32 devices: a whole 2x2x4 slice. The times are simulated.
32 devices in a mesh: parts: 2 (over x), dp: 16 (over z, y, core).
Axes of the slice: x: 2, y: 2, z: 4, core: 2. Of those that a mesh axis runs over, the one named last changes fastest.
Arguments:
- keys: bfloat16 [128, 512, 512], P(('parts', 'dp')), parts along dimension 0, may hold values from -6 to 6
- values: bfloat16 [128, 512, 512], P(('parts', 'dp')), parts along dimension 0, may hold values from -6 to 6
- lengths: int32 [128], P('parts'), parts along dimension 0, may hold values from 2 to 511
- anchor: int32 [128], P('parts'), parts along dimension 0, may hold values from 0 to 63, as said below
- queries: bfloat16 [128, 4096], P(('parts', 'dp')), parts along dimension 0, may hold values from -128 to 128
- new_keys: bfloat16 [128, 512], P(('parts', 'dp')), parts along dimension 0, may hold values from -6 to 6
- new_values: bfloat16 [128, 512], P(('parts', 'dp')), parts along dimension 0, may hold values from -6 to 6
Outputs:
- cache_keys: bfloat16 [128, 512, 512], P(('parts', 'dp')), parts along dimension 0
- cache_values: bfloat16 [128, 512, 512], P(('parts', 'dp')), parts along dimension 0
- attended: bfloat16 [128, 4096], P(('parts', 'dp')), parts along dimension 0
There are 2 independent parts, one for each index of `parts`. A program takes and returns all parts, laid end to end along the dimension named above; each array names one. Nothing has to cross between parts.
Inputs may be any that keep to these rules, and one draw needn't show every extreme that they name: anchor is a permutation of 0 to 63 with anchor[i] == i wherever anchor[i] is in the group of i; each group's requests that leave go to other groups, at most 2 leave and at most 2 enter each group, every group sends and receives at least one, and some group sends 2.
All inputs are finite; a program needn't handle non-finite values.
Results may differ from a plain program's by a relative error of at most 0.0051.
Values may be sent and summed in bfloat16 or wider, within the bound.
A program may use at most 64 MiB of HBM per device.

v0:
```python
import math

import jax
import jax.numpy as jnp
from jax import lax
from jax.sharding import PartitionSpec as P

HD = 128


def exclusive_rank(marked, group_total, slot_count):
    marked_grid = marked.reshape(group_total, slot_count).astype(jnp.int32)
    return (jnp.cumsum(marked_grid, axis=1) - marked_grid).reshape(-1)


def pick_rows(marked_grid, rank_grid, move_count):
    slot_count = marked_grid.shape[1]
    chosen = marked_grid[:, None, :] & (
        rank_grid[:, None, :] == jnp.arange(move_count, dtype=jnp.int32)[None, :, None]
    )
    where_slot = jnp.sum(
        chosen.astype(jnp.int32) * jnp.arange(slot_count, dtype=jnp.int32)[None, None, :], axis=2
    )
    return (where_slot, jnp.any(chosen, axis=2))


def pack_pieces(cache_rows, group_total):
    count, context, row_width = cache_rows.shape
    return cache_rows.reshape(count, group_total, context // group_total, row_width)


def unpack_pieces(pieces, context, row_width):
    count, group_total, piece_rows, piece_width = pieces.shape
    return pieces.reshape(count, context, row_width)


def place_token(cache_rows, token_row, length):
    positions = jnp.arange(cache_rows.shape[1], dtype=jnp.int32)
    written = (positions[None, :] == length[:, None])[:, :, None]
    return jnp.where(written, token_row[:, None, :], cache_rows)


def attend(queries_in, key_cache, value_cache, length):
    count, context, row_width = key_cache.shape
    heads_kv = row_width // HD
    per_group = queries_in.shape[1] // row_width
    query_heads = queries_in.reshape(count, heads_kv, per_group, HD)
    key_heads = key_cache.reshape(count, context, heads_kv, HD)
    value_heads = value_cache.reshape(count, context, heads_kv, HD)
    scores = jnp.einsum(
        "sjgd,scjd->sjgc", query_heads, key_heads, preferred_element_type=jnp.float32
    ) / math.sqrt(HD)
    positions = jnp.arange(context, dtype=jnp.int32)
    visible = (positions[None, :] <= length[:, None])[:, None, None, :]
    scores = jnp.where(visible, scores, jnp.float32(-1e30))
    largest = jnp.max(scores, axis=-1, keepdims=True)
    powers = jnp.where(visible, jnp.exp(scores - largest), jnp.float32(0.0))
    probs = (powers / jnp.sum(powers, axis=-1, keepdims=True)).astype(jnp.bfloat16)
    result = jnp.einsum("sjgc,scjd->sjgd", probs, value_heads, preferred_element_type=jnp.float32)
    return result.astype(jnp.bfloat16).reshape(count, -1)


def local(keys, values, lengths, anchor, queries, new_keys, new_values):
    group_total = lax.axis_size("dp")
    own_index = lax.axis_index("dp")
    slot_count, context, row_width = keys.shape
    move_count = (slot_count + 1) // 2
    slot_total = group_total * slot_count
    slot_ids = jnp.arange(slot_total, dtype=jnp.int32)
    moving = anchor // slot_count != slot_ids // slot_count
    target = jnp.zeros((slot_total,), jnp.int32).at[anchor].set(slot_ids)
    leaving = moving[target]
    out_rank = exclusive_rank(leaving, group_total, slot_count)
    in_rank = exclusive_rank(moving, group_total, slot_count)
    first_slot = own_index * slot_count
    own_length = lax.dynamic_slice_in_dim(lengths, first_slot, slot_count)
    positions = jnp.arange(context, dtype=jnp.int32)
    kept_mask = (positions[None, :] < own_length[:, None])[:, :, None]
    zero_value = jnp.zeros((), keys.dtype)
    masked_keys = jnp.where(kept_mask, keys, zero_value)
    masked_values = jnp.where(kept_mask, values, zero_value)
    own_leaving = lax.dynamic_slice_in_dim(leaving, first_slot, slot_count)
    own_out_rank = lax.dynamic_slice_in_dim(out_rank, first_slot, slot_count)
    send_slot, send_valid = pick_rows(own_leaving[None, :], own_out_rank[None, :], move_count)
    send_slot = send_slot[0]
    outgoing = (
        pack_pieces(masked_keys[send_slot], group_total),
        pack_pieces(masked_values[send_slot], group_total),
    )
    received = (
        lax.all_to_all(outgoing[0], "dp", split_axis=1, concat_axis=1, tiled=True),
        lax.all_to_all(outgoing[1], "dp", split_axis=1, concat_axis=1, tiled=True),
    )
    dest_local, dest_valid = pick_rows(
        moving.reshape(group_total, slot_count),
        in_rank.reshape(group_total, slot_count),
        move_count,
    )
    group_ids = jnp.arange(group_total, dtype=jnp.int32)
    source_slot = anchor[group_ids[:, None] * slot_count + dest_local]
    row_index = out_rank[source_slot] * group_total + source_slot // slot_count
    row_index = jnp.where(dest_valid, row_index, 0).T
    piece_rows, piece_width = (received[0].shape[2], received[0].shape[3])
    forward = (
        received[0].reshape(move_count * group_total, piece_rows, piece_width)[row_index],
        received[1].reshape(move_count * group_total, piece_rows, piece_width)[row_index],
    )
    arrived_keys = unpack_pieces(
        lax.all_to_all(forward[0], "dp", split_axis=1, concat_axis=1, tiled=True),
        context,
        row_width,
    )
    arrived_values = unpack_pieces(
        lax.all_to_all(forward[1], "dp", split_axis=1, concat_axis=1, tiled=True),
        context,
        row_width,
    )
    own_moving = lax.dynamic_slice_in_dim(moving, first_slot, slot_count)
    own_in_rank = lax.dynamic_slice_in_dim(in_rank, first_slot, slot_count)
    own_source = lax.dynamic_slice_in_dim(anchor, first_slot, slot_count)
    new_length = lengths[own_source]
    stack_index = jnp.where(
        own_moving, slot_count + own_in_rank, jnp.arange(slot_count, dtype=jnp.int32)
    )
    joined_keys = jnp.concatenate([masked_keys, arrived_keys], axis=0)[stack_index]
    joined_values = jnp.concatenate([masked_values, arrived_values], axis=0)[stack_index]
    cache_keys = place_token(joined_keys, new_keys, new_length)
    cache_values = place_token(joined_values, new_values, new_length)
    attended = attend(queries, cache_keys, cache_values, new_length)
    return (cache_keys, cache_values, attended)


def solution(mesh):
    in_specs = (
        P(("parts", "dp"), None, None),
        P(("parts", "dp"), None, None),
        P("parts"),
        P("parts"),
        P(("parts", "dp"), None),
        P(("parts", "dp"), None),
        P(("parts", "dp"), None),
    )
    out_specs = (
        P(("parts", "dp"), None, None),
        P(("parts", "dp"), None, None),
        P(("parts", "dp"), None),
    )
    return jax.shard_map(local, mesh=mesh, in_specs=in_specs, out_specs=out_specs, check_vma=False)
```

profile of v0, /device:TPU:13, one launch (start us, length us, event | category | flops | bytes accessed | tf_op | source)
XLA Modules:
  0.0 150.4 jit_solution(2146093264617581851)
XLA Ops:
  0.6 0.7 fusion.23
  1.3 0.7 compare_select_fusion.7
  2.0 0.8 scatter_custom_fusion
  2.8 0.8 gather_fusion.1
  3.6 0.2 reduce_window_sum.21
  3.8 0.1 reduce_window_sum.22
  4.1 0.1 fusion.22
  4.2 0.7 dynamic_slice.19
  5.0 3.4 %broadcast_select_fusion = (bf16[4,512,512]{2,1,0:T(8,128)(2,1)S(1)}, bf16[4,512,512]{2,1,0:T(8,128)(2,1)}) fusion(bf16[4,512,512]{2,1,0:T(8,128)(2,1)} %param.8, pred[4,512]{1,0:T(4,128)(4,1)S(1)} %iota_compare_fusion.1, bf16[4,512,512]{2,1,0:T(8,128)(2,1)} %param.7), kind=kLoop, calls=%fused_computation.22 | loop fusion | flops 2097152 | bytes 8390656 | tf_op jit(solution)/shard_map/jit(_where)/select_n | solution.py:81
  8.4 0.6 gather_fusion.7
  9.0 1.1 copy.67
  10.2 6.6 %all-to-all-start.2 = ((bf16[2,16,32,512]{3,2,0,1:T(8,128)(2,1)}), bf16[2,16,32,512]{3,2,0,1:T(8,128)(2,1)}, u32[]{:S(2)}, u32[]{:S(2)}) async-start(bf16[2,16,32,512]{3,2,0,1:T(8,128)(2,1)} %copy.67), calls=%async_computation.2 | async-start | bytes 2097152 | tf_op jit(solution)/shard_map/all_to_all | solution.py:92
  16.7 2.2 %gather_fusion.2 = bf16[2,512,512]{2,1,0:T(8,128)(2,1)S(1)} fusion(bf16[4,512,512]{2,1,0:T(8,128)(2,1)} %get-tuple-element.6, s32[1024]{0:T(1024)S(1)} %pad_clamp_fusion.4), kind=kCustom, calls=%fused_computation.2 | custom fusion | bytes 2097160 | tf_op jit(solution)/shard_map/gather | solution.py:87
  18.9 1.1 copy.54
  20.0 21.7 %all-to-all-done.2 = bf16[2,16,32,512]{3,2,0,1:T(8,128)(2,1)} async-done(((bf16[2,16,32,512]{3,2,0,1:T(8,128)(2,1)}), bf16[2,16,32,512]{3,2,0,1:T(8,128)(2,1)}, u32[]{:S(2)}, u32[]{:S(2)}) %all-to-all-start.2) | async-done | bytes 1048608 | tf_op jit(solution)/shard_map/all_to_all | solution.py:92
  41.7 4.9 %all-to-all-start = ((bf16[2,16,32,512]{3,2,0,1:T(8,128)(2,1)}), bf16[2,16,32,512]{3,2,0,1:T(8,128)(2,1)S(1)}, u32[]{:S(2)}, u32[]{:S(2)}) async-start(bf16[2,16,32,512]{3,2,0,1:T(8,128)(2,1)} %copy.54), calls=%async_computation | async-start | bytes 2097152 | tf_op jit(solution)/shard_map/all_to_all | solution.py:91
  46.6 0.1 and.47
  46.7 0.1 copy.56
  46.8 0.2 reduce_window_sum.23
  47.2 0.1 reshape.294
  47.3 0.7 gather_fusion.3
  48.1 0.1 reshape.293
  48.2 0.1 copy.59
  48.4 0.1 reshape.302
  48.5 0.7 gather_fusion.4
  49.3 0.1 copy.63
  49.6 2.4 %copy.68 = bf16[2,16,32,512]{3,2,1,0:T(8,128)(2,1)} copy(bf16[2,16,32,512]{3,2,0,1:T(8,128)(2,1)} %all-to-all-done.2) | data formatting | bytes 2097152 | tf_op jit(solution)/shard_map/all_to_all | solution.py:92
  52.0 2.8 %gather_fusion.8 = bf16[32,32,512]{2,1,0:T(8,128)(2,1)} fusion(bf16[32,32,512]{2,1,0:T(8,128)(2,1)} %bitcast.88, s32[1024]{0:T(1024)S(1)} %pad_clamp_fusion.1), kind=kCustom, calls=%fused_computation.8 | custom fusion | bytes 2097280 | tf_op jit(solution)/shard_map/gather | solution.py:106
  54.8 2.4 %copy.69 = bf16[2,16,32,512]{3,2,0,1:T(8,128)(2,1)} copy(bf16[2,16,32,512]{3,2,1,0:T(8,128)(2,1)} %bitcast.89) | data formatting | bytes 2097152 | tf_op jit(solution)/shard_map/gather | solution.py:106
  57.2 14.4 %all-to-all-done = bf16[2,16,32,512]{3,2,0,1:T(8,128)(2,1)S(1)} async-done(((bf16[2,16,32,512]{3,2,0,1:T(8,128)(2,1)}), bf16[2,16,32,512]{3,2,0,1:T(8,128)(2,1)S(1)}, u32[]{:S(2)}, u32[]{:S(2)}) %all-to-all-start) | async-done | bytes 1048608 | tf_op jit(solution)/shard_map/all_to_all | solution.py:91
  71.5 4.9 %all-to-all-start.3 = ((bf16[2,16,32,512]{3,2,0,1:T(8,128)(2,1)}), bf16[2,16,32,512]{3,2,0,1:T(8,128)(2,1)}, u32[]{:S(2)}, u32[]{:S(2)}) async-start(bf16[2,16,32,512]{3,2,0,1:T(8,128)(2,1)} %copy.69), calls=%async_computation.3 | async-start | bytes 2097152 | tf_op jit(solution)/shard_map/all_to_all | solution.py:114
  76.4 1.1 copy.55
  77.5 1.8 %gather_fusion.5 = bf16[32,32,512]{2,1,0:T(8,128)(2,1)S(1)} fusion(bf16[32,32,512]{2,1,0:T(8,128)(2,1)} %bitcast.86, s32[1024]{0:T(1024)S(1)} %pad_clamp_fusion.1), kind=kCustom, calls=%fused_computation.5 | custom fusion | bytes 2097280 | tf_op jit(solution)/shard_map/gather | solution.py:105
  79.4 1.1 copy.65
  80.5 20.9 %all-to-all-done.3 = bf16[2,16,32,512]{3,2,0,1:T(8,128)(2,1)} async-done(((bf16[2,16,32,512]{3,2,0,1:T(8,128)(2,1)}), bf16[2,16,32,512]{3,2,0,1:T(8,128)(2,1)}, u32[]{:S(2)}, u32[]{:S(2)}) %all-to-all-start.3) | async-done | bytes 1048608 | tf_op jit(solution)/shard_map/all_to_all | solution.py:114
  101.4 4.9 %all-to-all-start.1 = ((bf16[2,16,32,512]{3,2,0,1:T(8,128)(2,1)}), bf16[2,16,32,512]{3,2,0,1:T(8,128)(2,1)}, u32[]{:S(2)}, u32[]{:S(2)}) async-start(bf16[2,16,32,512]{3,2,0,1:T(8,128)(2,1)} %copy.65), calls=%async_computation.1 | async-start | bytes 2097152 | tf_op jit(solution)/shard_map/all_to_all | solution.py:109
  106.5 0.6 gather_fusion
  107.4 1.3 copy.70
  108.7 22.6 %all-to-all-done.1 = bf16[2,16,32,512]{3,2,0,1:T(8,128)(2,1)} async-done(((bf16[2,16,32,512]{3,2,0,1:T(8,128)(2,1)}), bf16[2,16,32,512]{3,2,0,1:T(8,128)(2,1)}, u32[]{:S(2)}, u32[]{:S(2)}) %all-to-all-start.1) | async-done | bytes 1048608 | tf_op jit(solution)/shard_map/all_to_all | solution.py:109
  131.3 1.4 copy.66
  132.8 0.5 copy-done.2
  133.3 3.0 %pad_maximum_fusion = (bf16[6,512,512]{2,1,0:T(8,128)(2,1)}, bf16[6,512,512]{2,1,0:T(8,128)(2,1)}) fusion(bf16[2,512,512]{2,1,0:T(8,128)(2,1)S(1)} %bitcast.83, bf16[4,512,512]{2,1,0:T(8,128)(2,1)S(1)} %copy-done.2, bf16[2,512,512]{2,1,0:T(8,128)(2,1)S(1)} %bitcast.82, bf16[4,512,512]{2,1,0:T(8,128)(2,1)S(1)} %get-tuple-element.5), kind=kLoop, calls=%fused_computation.12 | loop fusion | flops 3145728 | bytes 12582912 | tf_op jit(solution)/shard_map/concatenate | solution.py:125
  136.3 3.9 %gather_fusion.6 = bf16[4,512,512]{2,1,0:T(8,128)(2,1)} fusion(bf16[6,512,512]{2,1,0:T(8,128)(2,1)} %get-tuple-element.11, s32[1024]{0:T(1024)S(1)} %pad_clamp_fusion), kind=kCustom, calls=%fused_computation.6 | custom fusion | bytes 4194320 | tf_op jit(solution)/shard_map/gather | solution.py:125
  140.2 2.6 %gather_fusion.9 = bf16[4,512,512]{2,1,0:T(8,128)(2,1)S(1)} fusion(bf16[6,512,512]{2,1,0:T(8,128)(2,1)} %get-tuple-element.12, s32[1024]{0:T(1024)S(1)} %pad_clamp_fusion), kind=kCustom, calls=%fused_computation.9 | custom fusion | bytes 4194320 | tf_op jit(solution)/shard_map/gather | solution.py:126
  142.8 3.5 %broadcast_select_fusion.2 = (bf16[4,512,512]{2,1,0:T(8,128)(2,1)}, bf16[4,512,512]{2,1,0:T(8,128)(2,1)}) fusion(bf16[4,512,512]{2,1,0:T(8,128)(2,1)S(1)} %gather_fusion.9, pred[4,512]{1,0:T(4,128)(4,1)S(1)} %get-tuple-element.8, bf16[4,512]{1,0:T(4,128)(2,1)S(1)} %copy-done.3, bf16[4,512,512]{2,1,0:T(8,128)(2,1)} %gather_fusion.6, ...), kind=kLoop, calls=%fused_computation.24 | loop fusion | flops 2097152 | bytes 8398848 | tf_op jit(solution)/shard_map/jit(_where)/select_n | solution.py:40
  146.2 2.6 %fusion.27 = (f32[4,4,8]{2,1,0:T(4,128)S(1)}, f32[4,4,8,512]{3,2,1,0:T(8,128)S(1)}) fusion(pred[4,512]{1,0:T(4,128)(4,1)S(1)} %get-tuple-element.7, pred[4,512]{1,0:T(4,128)(4,1)S(1)} %get-tuple-element.8, bf16[4,4,128]{2,1,0:T(4,128)(2,1)S(1)} %broadcast_in_dim.127, bf16[1,4,32,128]{3,1,2,0:T(4,128)(2,1)S(1)} %bitcast.91, ...), kind=kOutput, calls=%fused_computation.91 | convolution fusion | flops 18153984 | bytes 2400768 | tf_op jit(solution)/shard_map/sub | solution.py:57
  148.8 0.9 fusion.14
  149.7 0.6 copy.104
  (50 shorter events, 1.5 us)
Async XLA Ops:
  10.2 31.5 %all-to-all-start.2 = ((bf16[2,16,32,512]{3,2,0,1:T(8,128)(2,1)}), bf16[2,16,32,512]{3,2,0,1:T(8,128)(2,1)}, u32[]{:S(2)}, u32[]{:S(2)}) async-start(bf16[2,16,32,512]{3,2,0,1:T(8,128)(2,1)} %copy.67), calls=%async_computation.2 | async-start | bytes 2097152 | tf_op jit(solution)/shard_map/all_to_all | solution.py:92
  18.9 28.4 %copy-start = (s32[64]{0:T(128)S(1)}, s32[64]{0:T(128)}, u32[]{:S(2)}) copy-start(s32[64]{0:T(128)} %param.10) | copy-start | bytes 772
  41.7 29.8 %all-to-all-start = ((bf16[2,16,32,512]{3,2,0,1:T(8,128)(2,1)}), bf16[2,16,32,512]{3,2,0,1:T(8,128)(2,1)S(1)}, u32[]{:S(2)}, u32[]{:S(2)}) async-start(bf16[2,16,32,512]{3,2,0,1:T(8,128)(2,1)} %copy.54), calls=%async_computation | async-start | bytes 2097152 | tf_op jit(solution)/shard_map/all_to_all | solution.py:91
  71.5 29.9 %all-to-all-start.3 = ((bf16[2,16,32,512]{3,2,0,1:T(8,128)(2,1)}), bf16[2,16,32,512]{3,2,0,1:T(8,128)(2,1)}, u32[]{:S(2)}, u32[]{:S(2)}) async-start(bf16[2,16,32,512]{3,2,0,1:T(8,128)(2,1)} %copy.69), calls=%async_computation.3 | async-start | bytes 2097152 | tf_op jit(solution)/shard_map/all_to_all | solution.py:114
  79.4 27.2 %copy-start.1 = (s32[64]{0:T(128)S(1)}, s32[64]{0:T(128)}, u32[]{:S(2)}) copy-start(s32[64]{0:T(128)} %param.9) | copy-start | bytes 772
  79.4 27.8 %copy-start.4 = (bf16[4,512]{1,0:T(4,128)(2,1)S(1)}, bf16[4,512]{1,0:T(4,128)(2,1)}, u32[]{:S(2)}) copy-start(bf16[4,512]{1,0:T(4,128)(2,1)} %param.12) | copy-start | bytes 12292
  79.4 27.8 %copy-start.3 = (bf16[4,512]{1,0:T(4,128)(2,1)S(1)}, bf16[4,512]{1,0:T(4,128)(2,1)}, u32[]{:S(2)}) copy-start(bf16[4,512]{1,0:T(4,128)(2,1)} %param.13) | copy-start | bytes 12292
  101.4 29.9 %all-to-all-start.1 = ((bf16[2,16,32,512]{3,2,0,1:T(8,128)(2,1)}), bf16[2,16,32,512]{3,2,0,1:T(8,128)(2,1)}, u32[]{:S(2)}, u32[]{:S(2)}) async-start(bf16[2,16,32,512]{3,2,0,1:T(8,128)(2,1)} %copy.65), calls=%async_computation.1 | async-start | bytes 2097152 | tf_op jit(solution)/shard_map/all_to_all | solution.py:109
  131.3 1.9 %copy-start.2 = (bf16[4,512,512]{2,1,0:T(8,128)(2,1)S(1)}, bf16[4,512,512]{2,1,0:T(8,128)(2,1)}, u32[]{:S(2)}) copy-start(bf16[4,512,512]{2,1,0:T(8,128)(2,1)} %get-tuple-element.6) | copy-start | bytes 6291460
  142.8 3.5 %copy-start.5 = (bf16[4,4096]{1,0:T(4,128)(2,1)S(1)}, bf16[4,4096]{1,0:T(4,128)(2,1)}, u32[]{:S(2)}) copy-start(bf16[4,4096]{1,0:T(4,128)(2,1)} %param.11) | copy-start | bytes 98308
where the time goes:
time: 151 us; the launch traced here: 150 us
  waiting for transfers between devices  79.6 us (53%)
  local copies, waits for them, and re-layouts  32.9 us (22%)
  starting transfers between devices  21.4 us (14%)
  other arithmetic  12.1 us (8%)
  matrix products  3.52 us (2%)
    all_to_all x1, waiting for transfers between devices, local(): lax.all_to_all(forward[0], 'dp', split_axis=1, concat_axis=1, tiled=True)  22.6 us
    all_to_all x1, waiting for transfers between devices, local(): lax.all_to_all(outgoing[1], 'dp', split_axis=1, concat_axis=1, tiled=True)  21.7 us
    all_to_all x1, waiting for transfers between devices, local(): lax.all_to_all(forward[1], 'dp', split_axis=1, concat_axis=1, tiled=True)  20.9 us
    all_to_all x1, waiting for transfers between devices, local(): lax.all_to_all(outgoing[0], 'dp', split_axis=1, concat_axis=1, tiled=True)  14.4 us
    all_to_all x1, starting transfers between devices, local(): lax.all_to_all(outgoing[1], 'dp', split_axis=1, concat_axis=1, tiled=True)  6.55 us
    gather x2, local copies, waits for them, and re-layouts, local(): received[1].reshape(move_count * group_total, piece_rows, piece_width)  5.19 us
    all_to_all x1, starting transfers between devices, local(): lax.all_to_all(outgoing[0], 'dp', split_axis=1, concat_axis=1, tiled=True)  4.94 us
    all_to_all x1, starting transfers between devices, local(): lax.all_to_all(forward[1], 'dp', split_axis=1, concat_axis=1, tiled=True)  4.94 us
  transfers between devices with their start and end apart: 4, of which 4 were waited for; matrix products, arithmetic and copies ran while one was open for 13% of the time, Pallas kernels for 0%

commit v1 on v0

v1 whole, which is shorter than its diff:
```python
import functools
import math

import jax
import jax.numpy as jnp
from jax import lax
from jax.experimental import pallas as pl
from jax.experimental.pallas import tpu as pltpu
from jax.sharding import PartitionSpec as P

HD = 128
ROWS = 16
CHUNKS = 2
MESH = pl.DeviceIdType.MESH
SEND, MOVED, ARRIVAL, LENGTH, FORWARD = 0, 4, 8, 12, 16


def plan_kernel(groups, slots, moves, anchor, lengths, meta, leaving, out_rank):
    me = lax.axis_index("dp")
    total = groups * slots

    def clear(i, c):
        leaving[i] = 0
        return c

    def mark(i, c):
        source = anchor[i]
        leaving[source] = (source // slots != i // slots).astype(jnp.int32)
        return c

    def rank(group, c):
        count = jnp.int32(0)
        for k in range(slots):
            out_rank[group * slots + k] = count
            count = count + leaving[group * slots + k]
        return c

    def forward(group, c):
        for e in range(moves):
            meta[FORWARD + group * moves + e] = 0
        count = jnp.int32(0)
        for k in range(slots):
            source = anchor[group * slots + k]
            moved = source // slots != group

            @pl.when(moved)
            def _():
                meta[FORWARD + group * moves + count] = source // slots * moves + out_rank[source]

            @pl.when(group == me)
            def _():
                meta[MOVED + k] = moved.astype(jnp.int32)
                meta[ARRIVAL + k] = jnp.where(moved, count, 0)
                meta[LENGTH + k] = lengths[source]

            count = count + moved.astype(jnp.int32)
        return c

    lax.fori_loop(0, total, clear, 0)
    lax.fori_loop(0, total, mark, 0)
    lax.fori_loop(0, groups, rank, 0)
    lax.fori_loop(0, groups, forward, 0)
    for e in range(slots):
        meta[SEND + e] = 0
    for k in range(slots):
        @pl.when(leaving[me * slots + k] == 1)
        def _():
            meta[SEND + out_rank[me * slots + k]] = k


def migrate_kernel(groups, slots, moves, chunks, meta, keys, values, out, *scratch):
    kv, send1, send2 = scratch[:3]
    recv1 = scratch[3 : 3 + chunks]
    load_sem, s1_sem, r1_sem, s2_sem, r2_sem, own_sem = scratch[3 + chunks :]
    me = lax.axis_index("dp")
    half = groups // 2
    depth = send1.shape[3]
    piece = depth * chunks

    loads = [
        pltpu.make_async_copy(keys, kv.at[pl.ds(0, slots)], load_sem.at[0]),
        pltpu.make_async_copy(values, kv.at[pl.ds(slots, slots)], load_sem.at[1]),
    ]
    for load in loads:
        load.start()
    barrier = pltpu.get_barrier_semaphore()

    def greet(d, c):
        pl.semaphore_signal(
            barrier, inc=1, device_id={"dp": lax.rem(me + d, groups)}, device_id_type=MESH
        )
        return c

    lax.fori_loop(1, groups, greet, 0)
    for load in loads:
        load.wait()
    pl.semaphore_wait(barrier, groups - 1)

    def hop1(chunk, peer, sender):
        return pltpu.make_async_remote_copy(
            src_ref=send1.at[chunk, peer],
            dst_ref=recv1[chunk].at[pl.ds(sender * moves, moves)],
            send_sem=s1_sem.at[chunk, peer],
            recv_sem=r1_sem.at[chunk, sender],
            device_id={"dp": peer},
            device_id_type=MESH,
        )

    def hop2(chunk, peer, sender):
        return pltpu.make_async_remote_copy(
            src_ref=send2.at[chunk, peer],
            dst_ref=out.at[sender, :, pl.ds(chunk * depth, depth)],
            send_sem=s2_sem.at[chunk, peer],
            recv_sem=r2_sem.at[chunk, sender],
            device_id={"dp": peer},
            device_id_type=MESH,
        )

    def own_copy(chunk):
        return pltpu.make_async_copy(
            send2.at[chunk, me], out.at[me, :, pl.ds(chunk * depth, depth)], own_sem.at[chunk]
        )

    def pack(chunk, peer, e):
        row = pl.multiple_of(lax.rem(peer, half) * piece + chunk * depth, ROWS)
        return kv[peer // half * slots + meta[SEND + e], pl.ds(row, depth)]

    for chunk in range(chunks):

        def start1(d, c):
            peer = lax.rem(me + d, groups)
            for e in range(moves):
                send1[chunk, peer, e] = pack(chunk, peer, e)
            hop1(chunk, peer, me).start()
            return c

        lax.fori_loop(1, groups, start1, 0)
        for e in range(moves):
            recv1[chunk][me * moves + e] = pack(chunk, me, e)

    for chunk in range(chunks):

        def wait1(d, c):
            sender = lax.rem(me + groups - d, groups)
            hop1(chunk, sender, sender).wait_recv()
            return c

        def fill(peer):
            for e in range(moves):
                send2[chunk, peer, e] = recv1[chunk][meta[FORWARD + peer * moves + e]]

        def start2(d, c):
            peer = lax.rem(me + d, groups)
            fill(peer)
            hop2(chunk, peer, me).start()
            return c

        lax.fori_loop(1, groups, wait1, 0)
        lax.fori_loop(1, groups, start2, 0)
        fill(me)
        own_copy(chunk).start()

    for chunk in range(chunks):

        def finish(d, c):
            peer = lax.rem(me + d, groups)
            sender = lax.rem(me + groups - d, groups)
            hop1(chunk, peer, me).wait_send()
            hop2(chunk, sender, sender).wait_recv()
            hop2(chunk, peer, me).wait_send()
            return c

        lax.fori_loop(1, groups, finish, 0)
        own_copy(chunk).wait()


def attend_kernel(meta, keys, values, arrived, queries, new_keys, new_values, out_k, out_v, out_a):
    slot = pl.program_id(0)
    moved = meta[MOVED + slot] == 1
    length = meta[LENGTH + slot]
    context, width = keys.shape[1:]
    per_group = queries.shape[1] // (width // HD)
    position = lax.broadcasted_iota(jnp.int32, (context, width), 0)

    def build(kind, own, token, out):
        @pl.when(moved)
        def _():
            out[0] = arrived[kind, :, 0].reshape(context, width)

        @pl.when(jnp.logical_not(moved))
        def _():
            out[0] = own[0]

        row = jnp.where(position == length, token[0], jnp.zeros((), out.dtype))
        out[0] = jnp.where(position < length, out[0], row)

    build(0, keys, new_keys, out_k)
    build(1, values, new_values, out_v)
    visible = lax.broadcasted_iota(jnp.int32, (per_group, context), 1) <= length
    for head in range(width // HD):
        lanes = slice(head * HD, (head + 1) * HD)
        rows = slice(head * per_group, (head + 1) * per_group)
        scores = lax.dot_general(
            queries[0, rows],
            out_k[0, :, lanes],
            (((1,), (1,)), ((), ())),
            preferred_element_type=jnp.float32,
        ) / math.sqrt(HD)
        scores = jnp.where(visible, scores, jnp.float32(-1e30))
        powers = jnp.exp(scores - jnp.max(scores, axis=-1, keepdims=True))
        powers = jnp.where(visible, powers, jnp.float32(0.0))
        probs = (powers / jnp.sum(powers, axis=-1, keepdims=True)).astype(jnp.bfloat16)
        result = jnp.dot(probs, out_v[0, :, lanes], preferred_element_type=jnp.float32)
        out_a[0, rows] = result.astype(out_a.dtype)


def local(keys, values, lengths, anchor, queries, new_keys, new_values):
    groups = lax.axis_size("dp")
    slots, context, width = keys.shape
    moves = (slots + 1) // 2
    half = groups // 2
    piece = context // half
    chunks = max(1, min(CHUNKS, piece // ROWS))
    depth = piece // chunks
    total = groups * slots
    kind = keys.dtype
    params = functools.partial(pltpu.CompilerParams, vmem_limit_bytes=40 << 20)
    smem = pl.BlockSpec(memory_space=pltpu.SMEM)
    hbm = pl.BlockSpec(memory_space=pl.ANY)

    meta = pl.pallas_call(
        functools.partial(plan_kernel, groups, slots, moves),
        out_shape=jax.ShapeDtypeStruct((FORWARD + groups * moves,), jnp.int32),
        in_specs=[smem, smem],
        out_specs=smem,
        scratch_shapes=[pltpu.SMEM((total,), jnp.int32), pltpu.SMEM((total,), jnp.int32)],
    )(anchor, lengths)

    dma = pltpu.SemaphoreType.DMA
    arrived = pl.pallas_call(
        functools.partial(migrate_kernel, groups, slots, moves, chunks),
        out_shape=jax.ShapeDtypeStruct((groups, moves, piece, width), kind),
        in_specs=[smem, hbm, hbm],
        out_specs=hbm,
        scratch_shapes=[
            pltpu.VMEM((2 * slots, context, width), kind),
            pltpu.VMEM((chunks, groups, moves, depth, width), kind),
            pltpu.VMEM((chunks, groups, moves, depth, width), kind),
        ]
        + [pltpu.VMEM((groups * moves, depth, width), kind) for _ in range(chunks)]
        + [dma((2,))]
        + [dma((chunks, groups)) for _ in range(4)]
        + [dma((chunks,))],
        compiler_params=params(collective_id=0, has_side_effects=True),
    )(meta, keys, values)
    arrived = arrived.reshape(2, half, moves, piece, width)

    heads = queries.shape[1] // HD
    cache = pl.BlockSpec((1, context, width), lambda i, m: (i, 0, 0))
    token = pl.BlockSpec((1, 1, width), lambda i, m: (i, 0, 0))
    query = pl.BlockSpec((1, heads, HD), lambda i, m: (i, 0, 0))
    landed = pl.BlockSpec(
        (2, half, 1, piece, width), lambda i, m: (0, 0, m[ARRIVAL + i], 0, 0)
    )
    cache_keys, cache_values, attended = pl.pallas_call(
        attend_kernel,
        out_shape=(
            jax.ShapeDtypeStruct(keys.shape, kind),
            jax.ShapeDtypeStruct(values.shape, kind),
            jax.ShapeDtypeStruct((slots, heads, HD), queries.dtype),
        ),
        grid_spec=pltpu.PrefetchScalarGridSpec(
            num_scalar_prefetch=1,
            grid=(slots,),
            in_specs=[cache, cache, landed, query, token, token],
            out_specs=(cache, cache, query),
        ),
        compiler_params=params(),
    )(
        meta,
        keys,
        values,
        arrived,
        queries.reshape(slots, heads, HD),
        new_keys[:, None],
        new_values[:, None],
    )
    return (cache_keys, cache_values, attended.reshape(queries.shape))


def solution(mesh):
    in_specs = (
        P(("parts", "dp"), None, None),
        P(("parts", "dp"), None, None),
        P("parts"),
        P("parts"),
        P(("parts", "dp"), None),
        P(("parts", "dp"), None),
        P(("parts", "dp"), None),
    )
    out_specs = (
        P(("parts", "dp"), None, None),
        P(("parts", "dp"), None, None),
        P(("parts", "dp"), None),
    )
    return jax.shard_map(local, mesh=mesh, in_specs=in_specs, out_specs=out_specs, check_vma=False)
```

time: 151 us -> 117 us (0.77)
  Pallas kernels: 0 us -> 109 us
  waiting for transfers between devices: 79.6 us -> 0 us
  local copies, waits for them, and re-layouts: 32.9 us -> 6.62 us
  starting transfers between devices: 21.4 us -> 0 us
  other arithmetic: 12.1 us -> 0 us
  matrix products: 3.52 us -> 0 us
    pallas_call x0 -> x3, Pallas kernels: none -> 109 us  [the longest x1 97.9 us: local(): pl.pallas_call(functools.partial(migrate_kernel, groups, slots, moves, ch...]
    all_to_all x4 -> x0, waiting for transfers between devices: 79.6 us -> none  [the longest x1 22.6 us: local(): lax.all_to_all(forward[0], 'dp', split_axis=1, concat_axis=1, tiled=True)]
    all_to_all x4 -> x0, starting transfers between devices: 21.4 us -> none  [the longest x1 6.55 us: local(): lax.all_to_all(outgoing[1], 'dp', split_axis=1, concat_axis=1, tiled=True)]
    gather x16 -> x0, local copies, waits for them, and re-layouts: 20.6 us -> none  [the longest x2 5.19 us: local(): received[1].reshape(move_count * group_total, piece_rows, piece_width)]
    select_n x10 -> x0, other arithmetic: 7.68 us -> none  [the longest x1 3.45 us: place_token(): return jnp.where(written, token_row[:, None, :], cache_rows)]
    all_to_all x4 -> x0, local copies, waits for them, and re-layouts: 6.2 us -> none  [the longest x1 2.37 us: local(): lax.all_to_all(outgoing[1], 'dp', split_axis=1, concat_axis=1, tiled=True)]
    unnamed x13 -> x8, local copies, waits for them, and re-layouts: 1.13 us -> 5.23 us
    concatenate x1 -> x0, other arithmetic: 3.01 us -> none  [local(): jnp.concatenate([masked_keys, arrived_keys], axis=0)[stack_index]]
  transfers between devices with their start and end apart: 4 -> 0, of which waited for: 4 -> 0; matrix products, arithmetic and copies ran while one was open for 13% -> 0% of each run, Pallas kernels for 0% -> 0%
where the time goes in v1:
time: 117 us; the launch traced here: 116 us
  Pallas kernels  109 us (93%)
  local copies, waits for them, and re-layouts  6.62 us (6%)
    pallas_call x1, Pallas kernels, local(): pl.pallas_call(functools.partial(migrate_kernel, groups, slots, moves, ch...  97.9 us
    pallas_call x1, Pallas kernels, local(): pl.pallas_call(attend_kernel, out_shape=(jax.ShapeDtypeStruct(keys.shape,...  7.69 us
    unnamed x8, local copies, waits for them, and re-layouts  5.23 us
    pallas_call x1, Pallas kernels, local(): pl.pallas_call(functools.partial(plan_kernel, groups, slots, moves), out_...  3.51 us

profile of v1, /device:TPU:13, one launch (start us, length us, event | category | flops | bytes accessed | tf_op | source)
XLA Modules:
  0.0 116.4 jit_solution(7554819886286176629)
XLA Ops:
  0.6 3.5 %shard_map.94.meta = s32[48]{0:T(128)} custom-call(s32[64]{0:T(128)} %anchor.1, s32[64]{0:T(128)} %lengths.1), custom_call_target="tpu_custom_call" | custom-call | tf_op jit(solution)/shard_map/pallas_call | solution.py:231
  4.1 0.7 copy.10.new_keys
  4.8 0.7 copy.11.new_values
  5.5 0.8 copy.17
  6.3 0.0 copy-start
  6.3 1.6 %copy-done = bf16[4,512,512]{2,1,0:T(8,128)(2,1)S(1)} copy-done((bf16[4,512,512]{2,1,0:T(8,128)(2,1)S(1)}, bf16[4,512,512]{2,1,0:T(8,128)(2,1)}, u32[]{:S(2)}) %copy-start) | copy-done | bytes 2097176
  7.9 0.0 copy-start.1
  7.9 1.6 %copy-done.1 = bf16[4,512,512]{2,1,0:T(8,128)(2,1)S(1)} copy-done((bf16[4,512,512]{2,1,0:T(8,128)(2,1)S(1)}, bf16[4,512,512]{2,1,0:T(8,128)(2,1)}, u32[]{:S(2)}) %copy-start.1) | copy-done | bytes 2097176
  9.5 0.0 copy-start.2
  9.5 0.7 copy-done.2
  10.1 97.9 %shard_map.95 = bf16[16,2,64,512]{3,2,1,0:T(8,128)(2,1)S(1)} custom-call(s32[48]{0:T(128)S(1)} %copy-done.2, bf16[4,512,512]{2,1,0:T(8,128)(2,1)S(1)} %copy-done, bf16[4,512,512]{2,1,0:T(8,128)(2,1)S(1)} %copy-done.1), custom_call_target="tpu_custom_call" | custom-call | tf_op jit(solution)/shard_map/pallas_call | solution.py:240
  108.1 7.7 %shard_map.96 = (bf16[4,512,512]{2,1,0:T(8,128)(2,1)}, bf16[4,512,512]{2,1,0:T(8,128)(2,1)}, bf16[4,32,128]{2,1,0:T(8,128)(2,1)S(1)}) custom-call(s32[48]{0:T(128)S(1)} %copy-done.2, bf16[4,512,512]{2,1,0:T(8,128)(2,1)S(1)} %copy-done, bf16[4,512,512]{2,1,0:T(8,128)(2,1)S(1)} %copy-done.1, bf16[2,8,2,64,512]{4,3,2,1,0:T(8,128)(2,1)S(1)} %bitcast.11, ...), custom_call_target="tpu_custom_call" | custom-call | tf_op jit(solution)/shard_map/pallas_call | solution.py:265
  115.8 0.6 copy.16
Async XLA Ops:
  6.3 1.6 %copy-start = (bf16[4,512,512]{2,1,0:T(8,128)(2,1)S(1)}, bf16[4,512,512]{2,1,0:T(8,128)(2,1)}, u32[]{:S(2)}) copy-start(bf16[4,512,512]{2,1,0:T(8,128)(2,1)} %keys.3) | copy-start | bytes 6291460
  7.9 1.6 %copy-start.1 = (bf16[4,512,512]{2,1,0:T(8,128)(2,1)S(1)}, bf16[4,512,512]{2,1,0:T(8,128)(2,1)}, u32[]{:S(2)}) copy-start(bf16[4,512,512]{2,1,0:T(8,128)(2,1)} %values.3) | copy-start | bytes 6291460
  9.5 0.7 copy-start.2

commit v2 on v1

v2 whole, which is shorter than its diff:
```python
import functools
import math

import jax
import jax.numpy as jnp
from jax import lax
from jax.experimental import pallas as pl
from jax.experimental.pallas import tpu as pltpu
from jax.sharding import PartitionSpec as P

HD = 128
ROWS = 16
CHUNKS = 2
MESH = pl.DeviceIdType.MESH


def moved_at(anchor, index):
    return (anchor[index] != index).astype(jnp.int32)


def rank_of(anchor, slot, slots):
    first = slot // slots * slots
    count = jnp.int32(0)
    for k in range(slots - 1):
        count = count + moved_at(anchor, first + k) * (first + k < slot).astype(jnp.int32)
    return count


def moved_slot(anchor, group, slots, e):
    found, count = jnp.int32(0), jnp.int32(0)
    for k in range(slots):
        moved = moved_at(anchor, group * slots + k)
        found = found + k * moved * (count == e).astype(jnp.int32)
        count = count + moved
    return found


def row_of(tokens, slot):
    rows = lax.broadcasted_iota(jnp.int32, tokens.shape, 0)
    picked = jnp.where(rows == slot, tokens[...].astype(jnp.float32), 0.0)
    return jnp.sum(picked, axis=0, keepdims=True).astype(tokens.dtype)


def placed(rows, token, length):
    position = lax.broadcasted_iota(jnp.int32, rows.shape, 0)
    tail = jnp.where(position == length, token, jnp.zeros((), rows.dtype))
    return jnp.where(position < length, rows, tail)


def attend(queries, keys, values, length):
    scores = lax.dot_general(
        queries, keys, (((1,), (1,)), ((), ())), preferred_element_type=jnp.float32
    ) / math.sqrt(HD)
    visible = lax.broadcasted_iota(jnp.int32, scores.shape, 1) <= length
    scores = jnp.where(visible, scores, jnp.float32(-1e30))
    powers = jnp.exp(scores - jnp.max(scores, axis=-1, keepdims=True))
    powers = jnp.where(visible, powers, jnp.float32(0.0))
    probs = (powers / jnp.sum(powers, axis=-1, keepdims=True)).astype(jnp.bfloat16)
    result = jnp.dot(probs, values, preferred_element_type=jnp.float32)
    return result.astype(jnp.bfloat16)


def migrate_kernel(
    groups, slots, moves, chunks, anchor, lengths, keys, values, queries, new_keys, new_values,
    out, kept, *scratch
):
    kv, send1, send2 = scratch[:3]
    recv1 = scratch[3 : 3 + chunks]
    load_sem, s1_sem, r1_sem, s2_sem, r2_sem, own_sem = scratch[3 + chunks :]
    me = lax.axis_index("dp")
    half = groups // 2
    depth = send1.shape[3]
    piece = depth * chunks

    loads = [
        pltpu.make_async_copy(keys, kv.at[pl.ds(0, slots)], load_sem.at[0]),
        pltpu.make_async_copy(values, kv.at[pl.ds(slots, slots)], load_sem.at[1]),
    ]
    for load in loads:
        load.start()
    barrier = pltpu.get_barrier_semaphore()

    def greet(d, c):
        pl.semaphore_signal(
            barrier, inc=1, device_id={"dp": lax.rem(me + d, groups)}, device_id_type=MESH
        )
        return c

    lax.fori_loop(1, groups, greet, 0)
    for load in loads:
        load.wait()
    pl.semaphore_wait(barrier, groups - 1)

    leave = [moved_slot(anchor, me, slots, e) for e in range(moves)]

    def hop1(chunk, peer, sender):
        return pltpu.make_async_remote_copy(
            src_ref=send1.at[chunk, peer],
            dst_ref=recv1[chunk].at[pl.ds(sender * moves, moves)],
            send_sem=s1_sem.at[chunk, peer],
            recv_sem=r1_sem.at[chunk, sender],
            device_id={"dp": peer},
            device_id_type=MESH,
        )

    def hop2(chunk, peer, sender):
        return pltpu.make_async_remote_copy(
            src_ref=send2.at[chunk, peer],
            dst_ref=out.at[sender, :, pl.ds(chunk * depth, depth)],
            send_sem=s2_sem.at[chunk, peer],
            recv_sem=r2_sem.at[chunk, sender],
            device_id={"dp": peer},
            device_id_type=MESH,
        )

    def own_copy(chunk):
        return pltpu.make_async_copy(
            send2.at[chunk, me], out.at[me, :, pl.ds(chunk * depth, depth)], own_sem.at[chunk]
        )

    def pack(chunk, peer, e):
        row = pl.multiple_of(lax.rem(peer, half) * piece + chunk * depth, ROWS)
        return kv[peer // half * slots + leave[e], pl.ds(row, depth)]

    for chunk in range(chunks):

        def start1(d, c):
            peer = lax.rem(me + d, groups)
            for e in range(moves):
                send1[chunk, peer, e] = pack(chunk, peer, e)
            hop1(chunk, peer, me).start()
            return c

        lax.fori_loop(1, groups, start1, 0)
        for e in range(moves):
            recv1[chunk][me * moves + e] = pack(chunk, me, e)

    def resident(slot, c):
        length = lengths[me * slots + slot]
        token_k, token_v = row_of(new_keys, slot), row_of(new_values, slot)
        per_group = queries.shape[1] // (kv.shape[2] // HD)
        for head in range(kv.shape[2] // HD):
            lanes = slice(head * HD, (head + 1) * HD)
            rows = slice(head * per_group, (head + 1) * per_group)
            kept[slot, rows] = attend(
                queries[slot, rows],
                placed(kv[slot, :, lanes], token_k[:, lanes], length),
                placed(kv[slots + slot, :, lanes], token_v[:, lanes], length),
                length,
            )
        return c

    lax.fori_loop(0, slots, resident, 0)

    for chunk in range(chunks):

        def wait1(d, c):
            sender = lax.rem(me + groups - d, groups)
            hop1(chunk, sender, sender).wait_recv()
            return c

        def fill(peer):
            for e in range(moves):
                source = anchor[peer * slots + moved_slot(anchor, peer, slots, e)]
                rank = jnp.minimum(rank_of(anchor, source, slots), moves - 1)
                send2[chunk, peer, e] = recv1[chunk][source // slots * moves + rank]

        def start2(d, c):
            peer = lax.rem(me + d, groups)
            fill(peer)
            hop2(chunk, peer, me).start()
            return c

        lax.fori_loop(1, groups, wait1, 0)
        lax.fori_loop(1, groups, start2, 0)
        fill(me)
        own_copy(chunk).start()

    for chunk in range(chunks):

        def finish(d, c):
            peer = lax.rem(me + d, groups)
            sender = lax.rem(me + groups - d, groups)
            hop1(chunk, peer, me).wait_send()
            hop2(chunk, sender, sender).wait_recv()
            hop2(chunk, peer, me).wait_send()
            return c

        lax.fori_loop(1, groups, finish, 0)
        own_copy(chunk).wait()


def arrival_of(anchor, me, slots, moves, slot):
    count = jnp.int32(0)
    for k in range(slots):
        count = count + moved_at(anchor, me * slots + k) * (k <= slot).astype(jnp.int32)
    return jnp.clip(count - 1, 0, moves - 1)


def place_kernel(
    slots, own, anchor, lengths, keys, values, arrived, kept, queries, new_keys, new_values,
    out_k, out_v, out_a
):
    slot = pl.program_id(0)
    index = own[0] * slots + slot
    length = lengths[anchor[index]]
    context, width = keys.shape[1:]
    per_group = queries.shape[1] // (width // HD)
    token_k, token_v = row_of(new_keys, slot), row_of(new_values, slot)

    @pl.when(anchor[index] == index)
    def _():
        out_k[0] = placed(keys[0], token_k, length)
        out_v[0] = placed(values[0], token_v, length)
        out_a[0] = kept[0]

    @pl.when(anchor[index] != index)
    def _():
        out_k[0] = placed(arrived[0, :, 0].reshape(context, width), token_k, length)
        out_v[0] = placed(arrived[1, :, 0].reshape(context, width), token_v, length)
        for head in range(width // HD):
            lanes = slice(head * HD, (head + 1) * HD)
            rows = slice(head * per_group, (head + 1) * per_group)
            out_a[0, rows] = attend(
                queries[0, rows], out_k[0, :, lanes], out_v[0, :, lanes], length
            )


def local(keys, values, lengths, anchor, queries, new_keys, new_values):
    groups = lax.axis_size("dp")
    slots, context, width = keys.shape
    moves = (slots + 1) // 2
    half = groups // 2
    piece = context // half
    chunks = max(1, min(CHUNKS, piece // ROWS))
    depth = piece // chunks
    kind = keys.dtype
    params = functools.partial(pltpu.CompilerParams, vmem_limit_bytes=56 << 20)
    smem = pl.BlockSpec(memory_space=pltpu.SMEM)
    hbm = pl.BlockSpec(memory_space=pl.ANY)

    dma = pltpu.SemaphoreType.DMA
    vmem = pl.BlockSpec(memory_space=pltpu.VMEM)
    heads = queries.shape[1] // HD
    tall = queries.reshape(slots, heads, HD)
    arrived, kept = pl.pallas_call(
        functools.partial(migrate_kernel, groups, slots, moves, chunks),
        out_shape=(
            jax.ShapeDtypeStruct((groups, moves, piece, width), kind),
            jax.ShapeDtypeStruct(tall.shape, tall.dtype),
        ),
        in_specs=[smem, smem, hbm, hbm, vmem, vmem, vmem],
        out_specs=(hbm, vmem),
        scratch_shapes=[
            pltpu.VMEM((2 * slots, context, width), kind),
            pltpu.VMEM((chunks, groups, moves, depth, width), kind),
            pltpu.VMEM((chunks, groups, moves, depth, width), kind),
        ]
        + [pltpu.VMEM((groups * moves, depth, width), kind) for _ in range(chunks)]
        + [dma((2,))]
        + [dma((chunks, groups)) for _ in range(4)]
        + [dma((chunks,))],
        compiler_params=params(collective_id=0, has_side_effects=True),
    )(anchor, lengths, keys, values, tall, new_keys, new_values)
    arrived = arrived.reshape(2, half, moves, piece, width)

    def landed(i, own, anchor, lengths):
        return (0, 0, arrival_of(anchor, own[0], slots, moves, i), 0, 0)

    cache = pl.BlockSpec((1, context, width), lambda i, *_: (i, 0, 0))
    token = pl.BlockSpec((slots, width), lambda i, *_: (0, 0))
    query = pl.BlockSpec((1, heads, HD), lambda i, *_: (i, 0, 0))
    cache_keys, cache_values, attended = pl.pallas_call(
        functools.partial(place_kernel, slots),
        out_shape=(
            jax.ShapeDtypeStruct(keys.shape, kind),
            jax.ShapeDtypeStruct(values.shape, kind),
            jax.ShapeDtypeStruct(tall.shape, tall.dtype),
        ),
        grid_spec=pltpu.PrefetchScalarGridSpec(
            num_scalar_prefetch=3,
            grid=(slots,),
            in_specs=[
                cache,
                cache,
                pl.BlockSpec((2, half, 1, piece, width), landed),
                query,
                query,
                token,
                token,
            ],
            out_specs=(cache, cache, query),
        ),
        compiler_params=params(),
    )(
        lax.axis_index("dp").reshape(1),
        anchor,
        lengths,
        keys,
        values,
        arrived,
        kept,
        tall,
        new_keys,
        new_values,
    )
    return (cache_keys, cache_values, attended.reshape(queries.shape))


def solution(mesh):
    in_specs = (
        P(("parts", "dp"), None, None),
        P(("parts", "dp"), None, None),
        P("parts"),
        P("parts"),
        P(("parts", "dp"), None),
        P(("parts", "dp"), None),
        P(("parts", "dp"), None),
    )
    out_specs = (
        P(("parts", "dp"), None, None),
        P(("parts", "dp"), None, None),
        P(("parts", "dp"), None),
    )
    return jax.shard_map(local, mesh=mesh, in_specs=in_specs, out_specs=out_specs, check_vma=False)
```

time: 117 us -> 112 us (0.957)
  local copies, waits for them, and re-layouts: 6.62 us -> 2.77 us
    unnamed x8 -> x2, local copies, waits for them, and re-layouts: 5.23 us -> 2.77 us
    pallas_call x2 -> x1, Pallas kernels: 11.2 us -> 8.96 us  [local(): pl.pallas_call(functools.partial(place_kernel, slots), out_shape=(jax.Sha...]
    broadcast_in_dim x2 -> x0, local copies, waits for them, and re-layouts: 1.39 us -> none  [the longest x1 0.7 us: local(): new_keys[:, None]]
where the time goes in v2:
time: 112 us; the launch traced here: 111 us
  Pallas kernels  108 us (96%)
  local copies, waits for them, and re-layouts  2.77 us (2%)
    pallas_call x1, Pallas kernels, local(): pl.pallas_call(functools.partial(migrate_kernel, groups, slots, moves, ch...  98.7 us
    pallas_call x1, Pallas kernels, local(): pl.pallas_call(functools.partial(place_kernel, slots), out_shape=(jax.Sha...  8.96 us
    unnamed x2, local copies, waits for them, and re-layouts  2.77 us

profile of v2, /device:TPU:13, one launch (start us, length us, event | category | flops | bytes accessed | tf_op | source)
XLA Modules:
  0.0 111.1 jit_solution(4996549366078001611)
XLA Ops:
  0.6 1.4 %copy.15 = bf16[1,4,32,128]{3,2,1,0:T(8,128)(2,1)} copy(bf16[1,4,32,128]{3,1,2,0:T(4,128)(2,1)} %bitcast.13) | data formatting | bytes 65536
  2.0 98.7 %shard_map.94 = (bf16[16,2,64,512]{3,2,1,0:T(8,128)(2,1)}, bf16[4,32,128]{2,1,0:T(8,128)(2,1)}) custom-call(s32[64]{0:T(128)} %anchor.3, s32[64]{0:T(128)} %lengths.3, bf16[4,512,512]{2,1,0:T(8,128)(2,1)} %keys.3, bf16[4,512,512]{2,1,0:T(8,128)(2,1)} %values.3, bf16[4,32,128]{2,1,0:T(8,128)(2,1)} %bitcast.11, bf16[4,512]{1,0:T(4,128)(2,1)} %new_keys.3, ...), custom_call_target="tpu_custom_call" | custom-call | tf_op jit(solution)/shard_map/pallas_call | solution.py:246
  100.8 9.0 %shard_map.95 = (bf16[4,512,512]{2,1,0:T(8,128)(2,1)}, bf16[4,512,512]{2,1,0:T(8,128)(2,1)}, bf16[4,32,128]{2,1,0:T(8,128)(2,1)}) custom-call(s32[1]{0:T(128)} %bitcast.own, s32[64]{0:T(128)} %anchor.3, s32[64]{0:T(128)} %lengths.3, bf16[4,512,512]{2,1,0:T(8,128)(2,1)} %keys.3, bf16[4,512,512]{2,1,0:T(8,128)(2,1)} %values.3, ...), custom_call_target="tpu_custom_call" | custom-call | tf_op jit(solution)/shard_map/pallas_call | solution.py:273
  109.7 1.4 %copy.14 = bf16[1,4,32,128]{3,1,2,0:T(4,128)(2,1)} copy(bf16[1,4,32,128]{3,2,1,0:T(8,128)(2,1)} %bitcast.15) | data formatting | bytes 65536
